TPU v7x, 128 devices: a whole 4x4x4 slice. The times are simulated.
128 devices in a mesh: replica: 8 (over z, x_lo), fsdp: 16 (over x_hi, y, core).
Axes of the slice: x: 4 (x_hi: 2, x_lo: 2; x = x_hi * 2 + x_lo), y: 4, z: 4, core: 2. Of those that a mesh axis runs over, the one named last changes fastest.
Arguments:
- gate_momentum: float32 [8, 1728, 4096], P('replica', 'fsdp'), may hold values from -24 to 24
- up_momentum: float32 [8, 1728, 4096], P('replica', 'fsdp'), may hold values from -24 to 24
- down_momentum: float32 [8, 320, 4096], P('replica', 'fsdp'), may hold values from -24 to 24
- gate_grad: bfloat16 [8, 1728, 4096], P('replica', 'fsdp'), may hold values from -6 to 6
- up_grad: bfloat16 [8, 1728, 4096], P('replica', 'fsdp'), may hold values from -6 to 6
- down_grad: bfloat16 [8, 320, 4096], P('replica', 'fsdp'), may hold values from -6 to 6
- gate_weight: bfloat16 [1728, 4096], P('fsdp'), may hold values from -6 to 6
- up_weight: bfloat16 [1728, 4096], P('fsdp'), may hold values from -6 to 6
- down_weight: bfloat16 [320, 4096], P('fsdp'), may hold values from -6 to 6
Outputs:
- gate_moment_next: float32 [8, 1728, 4096], P('replica', 'fsdp')
- up_moment_next: float32 [8, 1728, 4096], P('replica', 'fsdp')
- down_moment_next: float32 [8, 320, 4096], P('replica', 'fsdp')
- gate_gathered: bfloat16 [1728, 4096], replicated
- up_gathered: bfloat16 [1728, 4096], replicated
- down_gathered: bfloat16 [320, 4096], replicated
All inputs are finite; a program needn't handle non-finite values.
Results may differ from a plain program's by a relative error of at most 0.001.
Values may be sent and summed in bfloat16 or wider, within the bound.
A program may use at most 192 MiB of HBM per device.

v0:
```python
import jax
import jax.numpy as jnp
from jax import lax
from jax.sharding import PartitionSpec as P

TILE = 64
BAND = 8


def band_cosines():
    freq_row = jnp.arange(BAND).astype(jnp.float32)[:, None]
    position = jnp.arange(TILE).astype(jnp.float32)[None, :]
    cosines = jnp.sqrt(2.0 / TILE) * jnp.cos(
        jnp.pi * (2.0 * position + 1.0) * freq_row / (2.0 * TILE)
    )
    return jnp.where(freq_row == 0.0, cosines * jnp.sqrt(0.5), cosines)


def tile_transform(cosines):
    product = cosines[:, None, :, None] * cosines[None, :, None, :]
    return product.reshape(BAND * BAND, TILE * TILE)


def accumulate(momentum, gradient, transform):
    accumulated = 0.999 * momentum[0] + gradient[0].astype(jnp.float32)
    low_band = lax.dot_general(
        accumulated,
        transform,
        (((1,), (1,)), ((), ())),
        precision=lax.Precision.HIGHEST,
        preferred_element_type=jnp.float32,
    )
    removed = jnp.dot(
        low_band, transform, precision=lax.Precision.HIGHEST, preferred_element_type=jnp.float32
    )
    return ((accumulated - removed)[None], low_band.reshape(1, -1))


def refresh(weight, averaged, transform):
    update = jnp.dot(
        averaged, transform, precision=lax.Precision.HIGHEST, preferred_element_type=jnp.float32
    )
    root_mean = jnp.sqrt(jnp.mean(update * update, axis=1, keepdims=True) + 1e-06)
    return ((1.0 - 0.5 * 0.1) * weight.astype(jnp.float32) - 0.5 * update / root_mean).astype(
        jnp.bfloat16
    )


def on_device(
    gate_momentum,
    up_momentum,
    down_momentum,
    gate_grad,
    up_grad,
    down_grad,
    gate_weight,
    up_weight,
    down_weight,
):
    transform = tile_transform(band_cosines())
    gate_next, gate_flat = accumulate(gate_momentum, gate_grad, transform)
    up_next, up_flat = accumulate(up_momentum, up_grad, transform)
    down_next, down_flat = accumulate(down_momentum, down_grad, transform)
    replicas = lax.axis_size("replica")
    gate_parts, up_parts, down_parts = (
        lax.all_gather(gate_flat, "replica", axis=0, tiled=True),
        lax.all_gather(up_flat, "replica", axis=0, tiled=True),
        lax.all_gather(down_flat, "replica", axis=0, tiled=True),
    )
    gate_mean = jnp.sum(gate_parts, axis=0) / replicas
    up_mean = jnp.sum(up_parts, axis=0) / replicas
    down_mean = jnp.sum(down_parts, axis=0) / replicas
    gate_renewed = refresh(gate_weight, gate_mean.reshape(-1, BAND * BAND), transform)
    up_renewed = refresh(up_weight, up_mean.reshape(-1, BAND * BAND), transform)
    down_renewed = refresh(down_weight, down_mean.reshape(-1, BAND * BAND), transform)
    gate_whole, up_whole, down_whole = (
        lax.all_gather(gate_renewed, "fsdp", axis=0, tiled=True),
        lax.all_gather(up_renewed, "fsdp", axis=0, tiled=True),
        lax.all_gather(down_renewed, "fsdp", axis=0, tiled=True),
    )
    return (gate_next, up_next, down_next, gate_whole, up_whole, down_whole)


def solution(mesh):
    return jax.shard_map(
        on_device,
        mesh=mesh,
        in_specs=(
            P("replica", "fsdp", None),
            P("replica", "fsdp", None),
            P("replica", "fsdp", None),
            P("replica", "fsdp", None),
            P("replica", "fsdp", None),
            P("replica", "fsdp", None),
            P("fsdp", None),
            P("fsdp", None),
            P("fsdp", None),
        ),
        out_specs=(
            P("replica", "fsdp", None),
            P("replica", "fsdp", None),
            P("replica", "fsdp", None),
            P(),
            P(),
            P(),
        ),
        check_vma=False,
    )
```

profile of v0, /device:TPU:1, one launch (start us, length us, event | category | flops | bytes accessed | tf_op | source)
XLA Modules:
  0.0 317.5 jit_solution(15328584025532626966)
XLA Ops:
  7.2 0.0 all-gather.14.cloned.1.call-start
  7.2 0.1 multiply_select_fusion
  7.4 0.3 broadcast_multiply_fusion
  7.7 0.0 copy-start.3
  7.7 0.7 mul.357
  8.3 0.3 copy-done.3
  8.7 0.0 copy-start.7
  8.7 0.0 copy-start
  8.7 2.1 fusion.15
  10.7 0.1 reshape.237
  10.8 24.1 %all-gather.4 = f32[8,1,1280]{2,1,0:T(1,128)S(1)} all-gather(f32[1,1,1280]{2,1,0:T(1,128)S(1)} %reshape.237), channel_id=1, replica_groups=mesh['replica'=8,'fsdp'=16] {'replica'}, dimensions={0}, use_global_device_ids=true | all-gather | bytes 46080 | tf_op jit(solution)/shard_map/all_gather | solution.py:68
  35.0 0.1 div.87
  35.0 0.7 multiply_reduce_fusion.2
  35.8 0.0 copy-done.7
  35.8 0.8 fusion.20
  36.6 0.0 all-gather.14.cloned.1.call-update
  36.6 0.0 all-gather.12.cloned.1.call-start
  36.7 0.0 copy-done
  36.7 4.3 %fusion.3 = f32[108,64]{0,1:T(8,128)S(1)} fusion(f32[64,4096]{1,0:T(8,128)S(1)} %mul.357, f32[1,108,4096]{2,0,1:T(1,128)S(1)} %copy-done, bf16[1,108,4096]{2,1,0:T(8,128)(2,1)} %param.13), kind=kOutput, calls=%fused_computation.6 | convolution fusion | flops 341065728 | bytes 3730432 | tf_op jit(solution)/shard_map/dot_general | solution.py:26
  40.9 0.1 copy.33
  41.0 0.1 reshape.233
  41.1 22.2 %all-gather.2 = f32[8,1,6912]{2,1,0:T(1,128)S(1)} all-gather(f32[1,1,6912]{2,1,0:T(1,128)S(1)} %reshape.233), channel_id=1, replica_groups=mesh['replica'=8,'fsdp'=16] {'replica'}, dimensions={0}, use_global_device_ids=true | all-gather | bytes 248832 | tf_op jit(solution)/shard_map/all_gather | solution.py:67
  63.4 0.2 reduce_sum.56
  63.5 0.1 div.81
  63.6 0.0 copy-start.4
  63.6 1.7 multiply_reduce_fusion
  65.4 0.0 copy-done.4
  65.4 1.3 fusion.14
  66.7 0.0 all-gather.12.cloned.1.call-update
  66.7 0.0 all-gather.10.cloned.1.call-start
  66.8 4.8 %fusion.5 = f32[108,64]{0,1:T(8,128)S(1)} fusion(f32[64,4096]{1,0:T(8,128)S(1)} %mul.357, f32[1,108,4096]{2,0,1:T(1,128)} %param.9, bf16[1,108,4096]{2,1,0:T(8,128)(2,1)} %param.12), kind=kOutput, calls=%fused_computation.8 | convolution fusion | flops 341065728 | bytes 3730432 | tf_op jit(solution)/shard_map/dot_general | solution.py:26
  71.6 0.1 copy.32
  71.7 0.1 reshape.229
  71.8 23.8 %all-gather = f32[8,1,6912]{2,1,0:T(1,128)S(1)} all-gather(f32[1,1,6912]{2,1,0:T(1,128)S(1)} %reshape.229), channel_id=1, replica_groups=mesh['replica'=8,'fsdp'=16] {'replica'}, dimensions={0}, use_global_device_ids=true | all-gather | bytes 248832 | tf_op jit(solution)/shard_map/all_gather | solution.py:66
  95.6 0.2 reduce_sum.54
  95.8 0.1 div.76
  95.9 0.0 copy-start.5
  95.9 1.7 multiply_reduce_fusion.1
  97.7 0.0 copy-done.5
  97.7 1.3 fusion.13
  99.0 0.0 all-gather.10.cloned.1.call-update
  99.0 3.8 %fusion = f32[1,108,4096]{2,1,0:T(8,128)S(1)} fusion(f32[108,64]{0,1:T(8,128)S(1)} %fusion.3, f32[64,4096]{1,0:T(8,128)S(1)} %mul.357, bf16[1,108,4096]{2,1,0:T(8,128)(2,1)} %param.13, f32[1,108,4096]{2,0,1:T(1,128)S(1)} %copy-done), kind=kOutput, calls=%fused_computation.1 | convolution fusion | flops 341508096 | bytes 5499904 | tf_op jit(solution)/shard_map/dot_general | solution.py:33
  102.8 0.0 copy-start.6
  102.8 3.0 copy.35
  105.9 0.0 copy-done.6
  105.9 0.0 copy-start.1
  105.9 0.0 copy-start.2
  105.9 0.8 fusion.2
  106.6 1.1 copy.36
  107.7 0.0 copy-done.1
  107.7 0.2 copy-done.2
  107.8 2.6 fusion.1
  110.5 3.0 copy.34
  113.5 0.0 all-gather.14.cloned.1.call-done
  113.5 4.3 %reshape.240 = bf16[320,4096]{1,0:T(8,128)(2,1)} reshape(bf16[16,20,4096]{2,1,0:T(8,128)(2,1)} %all-gather.14.cloned.1.call-done) | data formatting | bytes 5242880
  117.8 79.7 %all-gather.12.cloned.1.call-done = bf16[16,108,4096]{2,1,0:T(8,128)(2,1)} async-done(((bf16[1,108,4096]{2,1,0:T(8,128)(2,1)}), bf16[16,108,4096]{2,1,0:T(8,128)(2,1)}) %all-gather.12.cloned.1.call-update) | async-done | bytes 14155792 | tf_op jit(solution)/shard_map/all_gather | solution.py:78
  197.4 13.4 %reshape.236 = bf16[1728,4096]{1,0:T(8,128)(2,1)} reshape(bf16[16,108,4096]{2,1,0:T(8,128)(2,1)} %all-gather.12.cloned.1.call-done) | data formatting | bytes 28311552
  210.9 87.0 %all-gather.10.cloned.1.call-done = bf16[16,108,4096]{2,1,0:T(8,128)(2,1)} async-done(((bf16[1,108,4096]{2,1,0:T(8,128)(2,1)}), bf16[16,108,4096]{2,1,0:T(8,128)(2,1)}) %all-gather.10.cloned.1.call-update) | async-done | bytes 14155792 | tf_op jit(solution)/shard_map/all_gather | solution.py:77
  297.8 13.2 %reshape.232 = bf16[1728,4096]{1,0:T(8,128)(2,1)} reshape(bf16[16,108,4096]{2,1,0:T(8,128)(2,1)} %all-gather.10.cloned.1.call-done) | data formatting | bytes 28311552
  (10 shorter events, 0.1 us)
Async XLA Ops:
  7.2 106.3 %all-gather.14.cloned.1.call-start = ((), (), s32[]{:S(2)}) async-start(), calls=%async_computation.2 | async-start | bytes 3342336 | tf_op jit(solution)/shard_map/all_gather | solution.py:79
  7.7 1.0 copy-start.3
  8.7 27.1 %copy-start.7 = (bf16[20,4096]{1,0:T(8,128)(2,1)S(1)}, bf16[20,4096]{1,0:T(8,128)(2,1)}, u32[]{:S(2)}) copy-start(bf16[20,4096]{1,0:T(8,128)(2,1)} %param.17) | copy-start | bytes 491524
  8.7 28.0 %copy-start = (f32[1,108,4096]{2,0,1:T(1,128)S(1)}, f32[1,108,4096]{2,0,1:T(1,128)}, u32[]{:S(2)}) copy-start(f32[1,108,4096]{2,0,1:T(1,128)} %param.10) | copy-start | bytes 5308420
  36.6 160.8 %all-gather.12.cloned.1.call-start = ((), (), s32[]{:S(2)}) async-start(), calls=%async_computation.1 | async-start | bytes 15597568 | tf_op jit(solution)/shard_map/all_gather | solution.py:78
  63.6 1.8 copy-start.4
  66.7 231.1 %all-gather.10.cloned.1.call-start = ((), (), s32[]{:S(2)}) async-start(), calls=%async_computation | async-start | bytes 15597568 | tf_op jit(solution)/shard_map/all_gather | solution.py:77
  95.9 1.8 copy-start.5
  102.8 3.0 copy-start.6
  105.9 1.8 copy-start.1
  105.9 2.0 copy-start.2
Sparse Core Ops, SparseCore 0:
  36.7 59.4 all-gather.13
  99.3 98.1 all-gather.11
  200.5 97.2 all-gather.9
where the time goes:
time: 318 us
  waiting for transfers between devices  167 us (53%)
  blocking collectives  70.2 us (22%)
  local copies, waits for them, and re-layouts  39.8 us (13%)
  matrix products  22.5 us (7%)
  between operations  13.9 us (4%)
  other arithmetic  4.27 us (1%)
    all_gather x1, waiting for transfers between devices, on_device(): lax.all_gather(gate_renewed, 'fsdp', axis=0, tiled=True)  87 us
    all_gather x1, waiting for transfers between devices, on_device(): lax.all_gather(up_renewed, 'fsdp', axis=0, tiled=True)  79.7 us
    unnamed x25, local copies, waits for them, and re-layouts  38.7 us
    all_gather x1, blocking collectives, on_device(): lax.all_gather(down_flat, 'replica', axis=0, tiled=True)  24.1 us
    all_gather x1, blocking collectives, on_device(): lax.all_gather(gate_flat, 'replica', axis=0, tiled=True)  23.8 us
    all_gather x1, blocking collectives, on_device(): lax.all_gather(up_flat, 'replica', axis=0, tiled=True)  22.2 us
    dot_general x3, matrix products, accumulate(): lax.dot_general(accumulated, transform, (((1,), (1,)), ((), ())), precisi...  11.1 us
    dot_general x3, matrix products, accumulate(): jnp.dot(low_band, transform, precision=lax.Precision.HIGHEST, preferred_e...  7.18 us
  transfers between devices with their start and end apart: 3, of which 2 were waited for; matrix products, arithmetic and copies ran while one was open for 15% of the time, Pallas kernels for 0%

commit v1 on v0

v1 whole, which is shorter than its diff:
```python
import functools

import jax
import jax.numpy as jnp
import ml_dtypes
import numpy as np
from jax import lax
from jax.experimental import pallas as pl
from jax.experimental.pallas import tpu as pltpu
from jax.sharding import PartitionSpec as P

TILE = 64
BAND = 8
COEFS = BAND * BAND
ENTRIES = TILE * TILE
F32 = jnp.float32
BF16 = jnp.bfloat16
MESH = pl.DeviceIdType.MESH
ANY = pl.BlockSpec(memory_space=pl.ANY)
VMEM = pl.BlockSpec(memory_space=pltpu.VMEM)

ROWS = 240
BAND_ROWS = 256


def split_transform():
    freq = np.arange(BAND, dtype=np.float64)[:, None]
    position = np.arange(TILE, dtype=np.float64)[None, :]
    cosines = np.sqrt(2.0 / TILE) * np.cos(np.pi * (2.0 * position + 1.0) * freq / (2.0 * TILE))
    cosines[0] *= np.sqrt(0.5)
    product = (cosines[:, None, :, None] * cosines[None, :, None, :]).reshape(COEFS, ENTRIES)
    head = product.astype(np.float32).astype(ml_dtypes.bfloat16)
    tail = (product - head.astype(np.float64)).astype(np.float32).astype(ml_dtypes.bfloat16)
    return np.concatenate([head, head, tail, tail], axis=0)


def head_tail(value):
    head = value.astype(BF16)
    return head, (value - head.astype(F32)).astype(BF16)


def fold_kernel(
    gate_m, up_m, down_m, gate_g, up_g, down_g, gate_w, up_w, down_w, transform,
    gate_n, up_n, down_n, packed, bands, rows, lows,
):
    step = 512
    chunks = [pl.ds(at, step) for at in range(0, ENTRIES, step)]

    def place(target, gate, up, down):
        odd = lax.rem(lax.axis_index("fsdp"), 2) == 1

        @pl.when(jnp.logical_not(odd))
        def _():
            target[0:108, :] = gate
            target[108:112, :] = down[16:20]
            target[112:220, :] = up
            target[220:224, :] = jnp.zeros_like(down[0:4])
            target[224:240, :] = down[0:16]

        @pl.when(odd)
        def _():
            target[0:4, :] = down[0:4]
            target[4:112, :] = gate
            target[112:116, :] = jnp.zeros_like(down[0:4])
            target[116:224, :] = up
            target[224:240, :] = down[4:20]

    def one(momentum, gradient, following):
        total = None
        for chunk in chunks:
            accumulated = 0.999 * momentum[0, :, chunk] + gradient[0, :, chunk].astype(F32)
            following[0, :, chunk] = accumulated
            for part in head_tail(accumulated):
                product = lax.dot_general(
                    part,
                    transform[COEFS : 3 * COEFS, chunk],
                    (((1,), (1,)), ((), ())),
                    preferred_element_type=F32,
                )
                total = product if total is None else total + product
        low = total[:, :COEFS] + total[:, COEFS:]
        head, tail = head_tail(low)
        both = jnp.concatenate([head, tail], axis=1)
        twice = jnp.concatenate([both, both], axis=1)
        for chunk in chunks:
            removed = jnp.dot(twice, transform[:, chunk], preferred_element_type=F32)
            following[0, :, chunk] = following[0, :, chunk] - removed
        return both.astype(F32)

    for chunk in chunks:
        place(
            rows,
            gate_w[:, chunk].astype(F32),
            up_w[:, chunk].astype(F32),
            down_w[:, chunk].astype(F32),
        )
        packed[:, chunk] = rows[...].astype(BF16)
    gate_low = one(gate_m, gate_g, gate_n)
    up_low = one(up_m, up_g, up_n)
    down_low = one(down_m, down_g, down_n)
    place(lows, gate_low, up_low, down_low)
    lows[ROWS:BAND_ROWS, :] = jnp.zeros((BAND_ROWS - ROWS, 2 * COEFS), F32)
    bands[...] = lows[...].astype(BF16)


def fold(arrays, transform):
    like = lambda a: jax.ShapeDtypeStruct(a.shape, a.dtype)
    return pl.pallas_call(
        fold_kernel,
        name="fold",
        out_shape=(
            like(arrays[0]),
            like(arrays[1]),
            like(arrays[2]),
            jax.ShapeDtypeStruct((ROWS, ENTRIES), BF16),
            jax.ShapeDtypeStruct((BAND_ROWS, 2 * COEFS), BF16),
        ),
        in_specs=[VMEM] * 10,
        out_specs=(VMEM,) * 5,
        scratch_shapes=[pltpu.VMEM((ROWS, 512), F32), pltpu.VMEM((BAND_ROWS, 2 * COEFS), F32)],
        compiler_params=pltpu.CompilerParams(vmem_limit_bytes=28 * 2**20),
    )(*arrays, transform)


UNIT_US, HOP_US, BANDS_US = 2.85, 1.0, 9.0
SIZE = {"E": 1.0, "D": 1.0, "H": 0.5, "C": 0.25}


def plan_messages():
    out = []
    band = lambda q: [("E", 0, q)] + [("D", q, k) for k in range(3)] + [("H", q), ("C", q)]
    for link, near in (("ym", 3), ("yp", 1)):
        for unit in band(0) + band(1) + [("E", dz, 1) for dz in (1, 2, 3)]:
            out.append((link, (0, near, unit), (0, 0, unit), None))
    for link, near, q, dz, half in (("ym", 3, 0, 1, 0), ("yp", 1, 1, 3, 1)):
        for unit in band(q) + [("E", dz, 1)]:
            out.append((link, (0, 2, unit), (0, near, unit), None))
        out.append((link, (0, 2, ("E", 2, 1)), (0, near, ("E", 2, 1)), half))
    for dy in range(4):
        for own, other in zip(band(0), band(1)):
            out.append(("xc", (1, dy, own), (0, dy, other), None))
            out.append(("xi", (1, dy, other), (1, dy, own), None))
    for link, dz, q, half in (("zm", 3, 0, 0), ("zp", 1, 1, 1)):
        for dy in (1, 2, 3):
            out.append((link, (0, dy, ("E", dz, 0)), (0, dy, ("E", 0, 0)), None))
            out.append((link, (0, dy, ("E", 2, 0)), (0, dy, ("E", dz, 0)), half))
        for dy in range(4):
            for each in (0, 1):
                out.append((link, (1, dy, ("E", dz, each)), (1, dy, ("E", 0, each)), None))
            out.append((link, (1, dy, ("E", 2, q)), (1, dy, ("E", dz, q)), None))
    return out


def plan():
    messages = plan_messages()
    users = {}
    for index, message in enumerate(messages):
        users.setdefault(message[2], []).append(index)
    cost = [SIZE[m[1][2][0]] * (0.5 if m[3] is not None else 1.0) * UNIT_US for m in messages]
    known = {}

    def tail(index):
        if index not in known:
            after = [tail(user) for user in users.get(messages[index][1], [])]
            known[index] = cost[index] + HOP_US + max(after + [0.0])
        return known[index]

    here = {}
    for message in messages:
        if message[2][:2] == (0, 0):
            here[message[2]] = BANDS_US if message[2][2][0] == "C" else 0.0
    free = dict.fromkeys(("ym", "yp", "xc", "xi", "zm", "zp"), 0.0)
    left = list(range(len(messages)))
    events = [(BANDS_US - 0.5, 0, -1)]
    while left:
        best = None
        for link in free:
            ready = [
                (max(free[link], here[messages[i][2]]), -tail(i), i)
                for i in left
                if messages[i][0] == link and messages[i][2] in here
            ]
            if ready:
                first = min(ready)[0]
                pick = min((r for r in ready if r[0] <= first), key=lambda r: r[1:])
                if best is None or pick[0] < best[0]:
                    best = (pick[0], link, pick[2])
        begin, link, index = best
        left.remove(index)
        free[link] = begin + cost[index]
        key = messages[index][1]
        arrive = free[link] + HOP_US
        events.append((max(here[messages[index][2]] + 0.01, begin - 1.2 * UNIT_US), 1, index))
        events.append((arrive, 0, index))
        here[key] = max(here.get(key, 0.0), arrive)
    return messages, sorted(events)


def spread_kernel(
    packed, bands, landing, coefs,
    peers, mine, received, own, band_sent, band_received, sent, sent_c, side_sent, side_sent_c,
    side_received, side_received_c,
):
    replica, shard = lax.axis_index("replica"), lax.axis_index("fsdp")
    z, lo = lax.div(replica, 2), lax.rem(replica, 2)
    hi, y, core = lax.div(shard, 8), lax.rem(lax.div(shard, 2), 4), lax.rem(shard, 2)
    device = lambda z, lo, hi, y, core: (2 * z + lo, 8 * hi + 2 * y + core)
    turn = lambda at, by: lax.rem(at + by, 4)
    target = {
        "ym": device(z, lo, hi, turn(y, 1), core),
        "yp": device(z, lo, hi, turn(y, 3), core),
        "xc": device(z, 1 - lo, 1 - hi, y, core),
        "xi": device(z, 1 - lo, hi, y, core),
        "zm": device(turn(z, 1), lo, hi, y, core),
        "zp": device(turn(z, 3), lo, hi, y, core),
    }
    sibling = device(z, lo, hi, y, 1 - core)
    fellows = [
        device(turn(z, dz), lo if same else 1 - lo, hi, y, core)
        for dz in range(4)
        for same in (True, False)
        if not (dz == 0 and same)
    ]

    barrier = pltpu.get_barrier_semaphore()
    partners = [target["ym"], target["yp"], target["xc"], sibling] + fellows
    for partner in partners:
        pl.semaphore_signal(barrier, 1, device_id=partner, device_id_type=MESH)
    pl.semaphore_wait(barrier, len(partners))

    def remote(source, dest, send, receive, to):
        return pltpu.make_async_remote_copy(
            src_ref=source, dst_ref=dest, send_sem=send, recv_sem=receive, device_id=to, device_id_type=MESH
        )

    block_at = {
        (dx, dy): 8 * (hi if dx == 0 else 1 - hi) + 2 * turn(y, dy) + core for dx in range(2) for dy in range(4)
    }
    parity = (lo, 1 - lo)

    def place(array_rows, key, half):
        kind = key[0]
        columns = slice(None) if half is None else pl.ds(half * (ENTRIES // 2), ENTRIES // 2)
        if kind == "E":
            start = 32 * turn(z, key[1]) + 16 * parity[key[2]]
        elif kind == "D":
            start = 128 + 48 * parity[key[1]] + 16 * key[2]
        elif kind == "H":
            start = 224
            columns = pl.ds(pl.multiple_of((ENTRIES // 2) * parity[key[1]], 128), ENTRIES // 2)
        else:
            return pl.ds(pl.multiple_of(128 * parity[key[1]], 16), 128), slice(None)
        return (pl.ds(start if isinstance(start, int) else pl.multiple_of(start, 16), 16), columns)

    def refs(key, half):
        dx, dy, unit = key
        rows, columns = place(None, unit, half)
        block = block_at[(dx, dy)]
        if unit[0] == "C":
            here = coefs.at[block, rows, columns]
            return (mine.at[rows, columns] if (dx, dy) == (0, 0) else here), here
        here = landing.at[block, rows, columns]
        return (packed.at[rows, columns] if (dx, dy) == (0, 0) else here), here

    for fellow in fellows:
        remote(bands, peers.at[replica], band_sent, band_received, fellow).start()

    messages, events = plan()
    me = block_at[(0, 0)]
    own_copy = pltpu.make_async_copy(packed, landing.at[me], own.at[0])
    own_coefs = pltpu.make_async_copy(mine, coefs.at[me], own.at[1])

    def send(index):
        link, key, key_there, half = messages[index]
        source, dest = refs(key_there, half)
        is_coefs = key[2][0] == "C"
        remote(source, dest, sent_c if is_coefs else sent, received.at[index], target[link]).start()

    def take(index):
        link, key, _, half = messages[index]
        _, dest = refs(key, half)
        is_coefs = key[2][0] == "C"
        remote(dest, dest, sent_c if is_coefs else sent, received.at[index], target[link]).wait_recv()
        remote(
            dest,
            dest,
            side_sent_c if is_coefs else side_sent,
            side_received_c if is_coefs else side_received,
            sibling,
        ).start()

    def average():
        peers[replica] = bands[...]
        remote(peers.at[0:7], peers.at[0:7], band_sent, band_received, sibling).wait_recv()
        total = peers[0].astype(F32)
        for each in range(1, 8):
            total = total + peers[each].astype(F32)
        averaged = (total[:, :COEFS] + total[:, COEFS:]) / 8.0
        square = jnp.sum(averaged * averaged, axis=1, keepdims=True) / ENTRIES
        head, tail = head_tail(-0.5 * averaged / jnp.sqrt(square + 1e-06))
        mine[...] = jnp.concatenate([head, tail], axis=1)
        own_coefs.start()
        remote(mine, coefs.at[me], side_sent_c, side_received_c, sibling).start()

    first = True
    for when, kind, index in events:
        if index >= 0 and kind == 1:
            send(index)
            continue
        if first:
            own_copy.start()
            remote(packed, landing.at[me], side_sent, side_received, sibling).start()
            first = False
        if index < 0:
            average()
        else:
            take(index)

    own_copy.wait()
    own_coefs.wait()
    remote(peers.at[0:7], peers.at[0:7], band_sent, band_received, sibling).wait_send()
    remote(landing.at[0:7], landing.at[0:7], sent, side_received, sibling).wait_send()
    remote(coefs.at[0:7], coefs.at[0:7], sent_c, side_received_c, sibling).wait_send()
    last = remote(landing.at[0:8], landing.at[0:8], side_sent, side_received, sibling)
    last_c = remote(coefs.at[0:8], coefs.at[0:8], side_sent_c, side_received_c, sibling)
    last.wait_send()
    last_c.wait_send()
    last.wait_recv()
    last_c.wait_recv()


def spread(packed, bands):
    dma = pltpu.SemaphoreType.DMA
    return pl.pallas_call(
        spread_kernel,
        name="spread",
        out_shape=(
            jax.ShapeDtypeStruct((16, ROWS, ENTRIES), BF16),
            jax.ShapeDtypeStruct((16, BAND_ROWS, 2 * COEFS), BF16),
        ),
        in_specs=[ANY, VMEM],
        out_specs=(ANY, ANY),
        scratch_shapes=[
            pltpu.VMEM((8, BAND_ROWS, 2 * COEFS), BF16),
            pltpu.VMEM((BAND_ROWS, 2 * COEFS), BF16),
            dma((len(plan_messages()),)),
            dma((2,)),
        ]
        + [dma] * 8,
        compiler_params=pltpu.CompilerParams(
            collective_id=0, has_side_effects=True, vmem_limit_bytes=8 * 2**20
        ),
    )(packed, bands)


QUAD = 4
WIDTH = 1024


def refresh_kernel(landing, coefs, transform, gate, up, down):
    low_half = lax.broadcasted_iota(jnp.int32, (8, 256), 0) < 4
    for at in range(0, WIDTH, 256):
        chunk = pl.ds(at, 256)
        gates, ups, downs = [], [], []

        def renewed(each):
            both = coefs[each, 0:ROWS, :]
            twice = jnp.concatenate([both, both], axis=1)
            update = jnp.dot(twice, transform[:, chunk], preferred_element_type=F32)
            return (1.0 - 0.5 * 0.1) * landing[each, :, chunk].astype(F32) + update

        for pair in range(QUAD // 2):
            even, odd = renewed(2 * pair), renewed(2 * pair + 1)
            join = lambda a, b: jnp.where(low_half, a, b)
            gates += [even[0:104], join(even[104:112], odd[0:8]), odd[8:112]]
            ups += [even[112:216], join(even[216:224], odd[112:120]), odd[120:224]]
            downs += [
                even[224:240],
                join(pltpu.roll(even[104:112], 4, 0), pltpu.roll(odd[0:8], 4, 0)),
                odd[224:240],
            ]
        gate[:, chunk] = jnp.concatenate(gates, axis=0).astype(BF16)
        up[:, chunk] = jnp.concatenate(ups, axis=0).astype(BF16)
        down[:, chunk] = jnp.concatenate(downs, axis=0).astype(BF16)


def refresh(landing, coefs, transform):
    whole = lambda rows: jax.ShapeDtypeStruct((16 * rows, ENTRIES), BF16)
    out = lambda rows: pl.BlockSpec((QUAD * rows, WIDTH), lambda g, c: (g, c))
    return pl.pallas_call(
        refresh_kernel,
        name="refresh",
        grid=(16 // QUAD, ENTRIES // WIDTH),
        out_shape=(whole(108), whole(108), whole(20)),
        in_specs=[
            pl.BlockSpec((QUAD, ROWS, WIDTH), lambda g, c: (g, 0, c)),
            pl.BlockSpec((QUAD, BAND_ROWS, 2 * COEFS), lambda g, c: (g, 0, 0)),
            pl.BlockSpec((4 * COEFS, WIDTH), lambda g, c: (0, c)),
        ],
        out_specs=(out(108), out(108), out(20)),
        compiler_params=pltpu.CompilerParams(vmem_limit_bytes=20 * 2**20),
    )(landing, coefs, transform)


def on_device(*arrays):
    transform = jnp.asarray(split_transform())
    gate_next, up_next, down_next, packed, bands = fold(arrays, transform)
    landing, coefs = spread(packed, bands)
    gate_whole, up_whole, down_whole = refresh(landing, coefs, transform)
    return (gate_next, up_next, down_next, gate_whole, up_whole, down_whole)


def solution(mesh):
    by_replica, by_shard = P("replica", "fsdp", None), P("fsdp", None)
    return jax.shard_map(
        on_device,
        mesh=mesh,
        in_specs=(by_replica,) * 6 + (by_shard,) * 3,
        out_specs=(by_replica,) * 3 + (P(),) * 3,
        check_vma=False,
    )
```

time: 318 us -> 135 us (0.42)
  waiting for transfers between devices: 167 us -> 0 us
  Pallas kernels: 0 us -> 100 us
  blocking collectives: 70.2 us -> 0 us
  matrix products: 22.5 us -> 0 us
  between operations: 13.9 us -> 0.77 us
  local copies, waits for them, and re-layouts: 39.8 us -> 33.5 us
  other arithmetic: 4.27 us -> 0 us
    all_gather x3 -> x0, waiting for transfers between devices: 167 us -> none  [the longest x1 87 us: on_device(): lax.all_gather(gate_renewed, 'fsdp', axis=0, tiled=True)]
    pallas_call x0 -> x3, Pallas kernels: none -> 100 us  [the longest x1 77.1 us: spread(): pl.pallas_call(spread_kernel, name='spread', out_shape=(jax.ShapeDtypeStr...]
    all_gather x3 -> x0, blocking collectives: 70.2 us -> none  [the longest x1 24.1 us: on_device(): lax.all_gather(down_flat, 'replica', axis=0, tiled=True)]
    dot_general x9 -> x0, matrix products: 22.5 us -> none  [the longest x3 11.1 us: accumulate(): lax.dot_general(accumulated, transform, (((1,), (1,)), ((), ())), precisi...]
    unnamed x25 -> x26, local copies, waits for them, and re-layouts: 38.7 us -> 33.5 us
    unnamed x3 -> x0, other arithmetic: 3.41 us -> none
  transfers between devices with their start and end apart: 3 -> 0, of which waited for: 2 -> 0; matrix products, arithmetic and copies ran while one was open for 15% -> 0% of each run, Pallas kernels for 0% -> 0%
where the time goes in v1:
time: 135 us
  Pallas kernels  100 us (74%)
  local copies, waits for them, and re-layouts  33.5 us (25%)
    pallas_call x1, Pallas kernels, spread(): pl.pallas_call(spread_kernel, name='spread', out_shape=(jax.ShapeDtypeStr...  77.1 us
    unnamed x26, local copies, waits for them, and re-layouts  33.5 us
    pallas_call x1, Pallas kernels, refresh(): pl.pallas_call(refresh_kernel, name='refresh', grid=(16 // QUAD, ENTRIES...  17 us
    pallas_call x1, Pallas kernels, fold(): pl.pallas_call(fold_kernel, name='fold', out_shape=(like(arrays[0]), like...  6.35 us

profile of v1, /device:TPU:1, one launch (start us, length us, event | category | flops | bytes accessed | tf_op | source)
XLA Modules:
  0.0 134.7 jit_solution(5326224659835859340)
XLA Ops:
  0.6 0.0 copy-start.9
  0.6 1.3 copy.18.down_m
  1.9 0.0 copy-start.4
  2.0 0.0 copy-start.5
  2.0 0.0 copy-start.6
  2.0 2.9 %copy.16.gate_m = f32[1,108,4096]{2,1,0:T(8,128)S(1)} copy(f32[1,108,4096]{2,0,1:T(1,128)} %param.10) | data formatting | bytes 3538944 | tf_op args[0]
  4.9 0.0 copy-done.9
  4.9 0.0 copy-start.2
  5.0 0.0 copy-start.3
  5.0 0.0 copy-start.7
  5.0 0.0 copy-start.8
  5.0 1.3 copy.17.up_m
  6.3 0.0 copy-done.4
  6.3 0.0 copy-done.5
  6.3 0.0 copy-done.6
  6.3 0.2 copy-done.2
  6.5 0.2 copy-done.3
  6.8 0.0 copy-done.7
  6.8 0.1 copy-done.8
  6.8 6.3 %fold.1 = (f32[1,108,4096]{2,1,0:T(8,128)S(1)}, f32[1,108,4096]{2,1,0:T(8,128)S(1)}, f32[1,20,4096]{2,1,0:T(8,128)S(1)}, bf16[240,4096]{1,0:T(8,128)(2,1)S(1)}, bf16[256,128]{1,0:T(8,128)(2,1)S(1)}) custom-call(f32[1,108,4096]{2,1,0:T(8,128)S(1)} %copy.16.gate_m, f32[1,108,4096]{2,1,0:T(8,128)S(1)} %copy.17.up_m, f32[1,20,4096]{2,1,0:T(8,128)S(1)} %copy.18.down_m, ...), custom_call_target="tpu_custom_call" | custom-call | tf_op jit(solution)/shard_map/fold/pallas_call | solution.py:108
  13.2 3.0 %copy.19 = f32[1,108,4096]{2,0,1:T(1,128)} copy(f32[1,108,4096]{2,1,0:T(8,128)S(1)} %get-tuple-element.26) | data formatting | bytes 3538944
  16.2 1.1 copy.21
  17.3 3.0 %copy.20 = f32[1,108,4096]{2,0,1:T(1,128)} copy(f32[1,108,4096]{2,1,0:T(8,128)S(1)} %get-tuple-element.27) | data formatting | bytes 3538944
  20.3 77.1 %spread.1 = (bf16[16,240,4096]{2,1,0:T(8,128)(2,1)S(1)}, bf16[16,256,128]{2,1,0:T(8,128)(2,1)S(1)}) custom-call(bf16[240,4096]{1,0:T(8,128)(2,1)S(1)} %get-tuple-element.19.packed, bf16[256,128]{1,0:T(8,128)(2,1)S(1)} %get-tuple-element.20.bands), custom_call_target="tpu_custom_call" | custom-call | tf_op jit(solution)/shard_map/spread/pallas_call | solution.py:334
  97.4 0.0 copy-start
  97.4 10.4 %copy-done = bf16[16,240,4096]{2,1,0:T(8,128)(2,1)} copy-done((bf16[16,240,4096]{2,1,0:T(8,128)(2,1)}, bf16[16,240,4096]{2,1,0:T(8,128)(2,1)S(1)}, u32[]{:S(2)}) %copy-start) | copy-done | bytes 31457304
  107.8 0.0 copy-start.1
  107.8 9.9 %copy-done.1 = bf16[16,240,4096]{2,1,0:T(8,128)(2,1)S(1)} copy-done((bf16[16,240,4096]{2,1,0:T(8,128)(2,1)S(1)}, bf16[16,240,4096]{2,1,0:T(8,128)(2,1)}, u32[]{:S(2)}) %copy-start.1) | copy-done | bytes 31457304
  117.7 17.0 %refresh.1 = (bf16[1728,4096]{1,0:T(8,128)(2,1)}, bf16[1728,4096]{1,0:T(8,128)(2,1)}, bf16[320,4096]{1,0:T(8,128)(2,1)}) custom-call(bf16[16,240,4096]{2,1,0:T(8,128)(2,1)S(1)} %copy-done.1, bf16[16,256,128]{2,1,0:T(8,128)(2,1)S(1)} %get-tuple-element.22.coefs, bf16[256,4096]{1,0:T(8,128)(2,1)S(1)} %copy-done.2), custom_call_target="tpu_custom_call" | custom-call | tf_op jit(solution)/shard_map/refresh/pallas_call | solution.py:390
Async XLA Ops:
  0.6 4.3 %copy-start.9 = (f32[1,108,4096]{2,0,1:T(1,128)S(1)}, f32[1,108,4096]{2,0,1:T(1,128)}, u32[]{:S(2)}) copy-start(f32[1,108,4096]{2,0,1:T(1,128)} %param.11) | copy-start | bytes 5308420
  1.9 4.4 %copy-start.4 = (bf16[1,108,4096]{2,1,0:T(8,128)(2,1)S(1)}, bf16[1,108,4096]{2,1,0:T(8,128)(2,1)}, u32[]{:S(2)}) copy-start(bf16[1,108,4096]{2,1,0:T(8,128)(2,1)} %up_g.1) | copy-start | bytes 2654212
  2.0 4.4 %copy-start.5 = (bf16[108,4096]{1,0:T(8,128)(2,1)S(1)}, bf16[108,4096]{1,0:T(8,128)(2,1)}, u32[]{:S(2)}) copy-start(bf16[108,4096]{1,0:T(8,128)(2,1)} %gate_w.1) | copy-start | bytes 2654212
  2.0 4.4 %copy-start.6 = (bf16[108,4096]{1,0:T(8,128)(2,1)S(1)}, bf16[108,4096]{1,0:T(8,128)(2,1)}, u32[]{:S(2)}) copy-start(bf16[108,4096]{1,0:T(8,128)(2,1)} %up_w.1) | copy-start | bytes 2654212
  4.9 1.6 %copy-start.2 = (bf16[256,4096]{1,0:T(8,128)(2,1)S(1)}, bf16[256,4096]{1,0:T(8,128)(2,1)}, u32[]{:S(2)}) copy-start(bf16[256,4096]{1,0:T(8,128)(2,1)} %constant.2.clone.transform) | copy-start | bytes 6291460
  5.0 1.8 %copy-start.3 = (bf16[1,108,4096]{2,1,0:T(8,128)(2,1)S(1)}, bf16[1,108,4096]{2,1,0:T(8,128)(2,1)}, u32[]{:S(2)}) copy-start(bf16[1,108,4096]{2,1,0:T(8,128)(2,1)} %gate_g.1) | copy-start | bytes 2654212
  5.0 1.8 %copy-start.7 = (bf16[1,20,4096]{2,1,0:T(8,128)(2,1)S(1)}, bf16[1,20,4096]{2,1,0:T(8,128)(2,1)}, u32[]{:S(2)}) copy-start(bf16[1,20,4096]{2,1,0:T(8,128)(2,1)} %down_g.1) | copy-start | bytes 491524
  5.0 1.9 %copy-start.8 = (bf16[20,4096]{1,0:T(8,128)(2,1)S(1)}, bf16[20,4096]{1,0:T(8,128)(2,1)}, u32[]{:S(2)}) copy-start(bf16[20,4096]{1,0:T(8,128)(2,1)} %down_w.1) | copy-start | bytes 491524
  97.4 10.4 %copy-start = (bf16[16,240,4096]{2,1,0:T(8,128)(2,1)}, bf16[16,240,4096]{2,1,0:T(8,128)(2,1)S(1)}, u32[]{:S(2)}) copy-start(bf16[16,240,4096]{2,1,0:T(8,128)(2,1)S(1)} %get-tuple-element.21.landing) | copy-start | bytes 94371840
  107.8 9.9 %copy-start.1 = (bf16[16,240,4096]{2,1,0:T(8,128)(2,1)S(1)}, bf16[16,240,4096]{2,1,0:T(8,128)(2,1)}, u32[]{:S(2)}) copy-start(bf16[16,240,4096]{2,1,0:T(8,128)(2,1)} %copy-done) | copy-start | bytes 94371840

commit v2 on v1

v2 whole, which is shorter than its diff:
```python
import functools

import jax
import jax.numpy as jnp
import ml_dtypes
import numpy as np
from jax import lax
from jax.experimental import pallas as pl
from jax.experimental.pallas import tpu as pltpu
from jax.sharding import PartitionSpec as P

TILE = 64
BAND = 8
COEFS = BAND * BAND
ENTRIES = TILE * TILE
F32 = jnp.float32
BF16 = jnp.bfloat16
MESH = pl.DeviceIdType.MESH
ANY = pl.BlockSpec(memory_space=pl.ANY)
VMEM = pl.BlockSpec(memory_space=pltpu.VMEM)

ROWS = 240
BAND_ROWS = 256
EARLY = 128
STEP = 512


def split_transform():
    freq = np.arange(BAND, dtype=np.float64)[:, None]
    position = np.arange(TILE, dtype=np.float64)[None, :]
    cosines = np.sqrt(2.0 / TILE) * np.cos(np.pi * (2.0 * position + 1.0) * freq / (2.0 * TILE))
    cosines[0] *= np.sqrt(0.5)
    product = (cosines[:, None, :, None] * cosines[None, :, None, :]).reshape(COEFS, ENTRIES)
    head = product.astype(np.float32).astype(ml_dtypes.bfloat16)
    tail = (product - head.astype(np.float64)).astype(np.float32).astype(ml_dtypes.bfloat16)
    return np.concatenate([head, head, tail, tail], axis=0)


def in_hbm(*arrays):
    return tuple(pltpu.with_memory_space_constraint(a, pltpu.HBM) for a in arrays)


def head_tail(value):
    head = value.astype(BF16)
    return head, (value - head.astype(F32)).astype(BF16)


UNIT_US, HOP_US, BANDS_US = 2.85, 3.0, 22.0
FOLD_US, REMOVE_US = 14.0, 24.0
SIZE = {"E": 1.0, "D": 1.0, "H": 0.5, "C": 0.25}


def plan_messages():
    out = []
    band = lambda q: [("E", 0, q)] + [("D", q, k) for k in range(3)] + [("H", q), ("C", q)]
    for link, near in (("ym", 3), ("yp", 1)):
        for unit in band(0) + band(1) + [("E", dz, 1) for dz in (1, 2, 3)]:
            out.append((link, (0, near, unit), (0, 0, unit), None))
    for link, near, q, dz, half in (("ym", 3, 0, 1, 0), ("yp", 1, 1, 3, 1)):
        for unit in band(q) + [("E", dz, 1)]:
            out.append((link, (0, 2, unit), (0, near, unit), None))
        out.append((link, (0, 2, ("E", 2, 1)), (0, near, ("E", 2, 1)), half))
    for dy in range(4):
        for own, other in zip(band(0), band(1)):
            out.append(("xc", (1, dy, own), (0, dy, other), None))
            out.append(("xi", (1, dy, other), (1, dy, own), None))
    for link, dz, q, half in (("zm", 3, 0, 0), ("zp", 1, 1, 1)):
        for dy in (1, 2, 3):
            out.append((link, (0, dy, ("E", dz, 0)), (0, dy, ("E", 0, 0)), None))
            out.append((link, (0, dy, ("E", 2, 0)), (0, dy, ("E", dz, 0)), half))
        for dy in range(4):
            for each in (0, 1):
                out.append((link, (1, dy, ("E", dz, each)), (1, dy, ("E", 0, each)), None))
            out.append((link, (1, dy, ("E", 2, q)), (1, dy, ("E", dz, q)), None))
    return out


def plan():
    messages = plan_messages()
    users = {}
    for index, message in enumerate(messages):
        users.setdefault(message[2], []).append(index)
    cost = [SIZE[m[1][2][0]] * (0.5 if m[3] is not None else 1.0) * UNIT_US for m in messages]
    known = {}

    def tail(index):
        if index not in known:
            after = [tail(user) for user in users.get(messages[index][1], [])]
            known[index] = cost[index] + HOP_US + max(after + [0.0])
        return known[index]

    here = {}
    for message in messages:
        if message[2][:2] == (0, 0):
            here[message[2]] = BANDS_US if message[2][2][0] == "C" else 0.0
    free = dict.fromkeys(("ym", "yp", "xc", "xi", "zm", "zp"), 0.0)
    left = list(range(len(messages)))
    steps = 3 * (ENTRIES // STEP)
    events = [(FOLD_US * (i + 0.5) / steps, 2, i) for i in range(steps)]
    events += [(FOLD_US + 0.1, 2, steps), (BANDS_US - 0.5, 2, steps + 1)]
    events += [(REMOVE_US + FOLD_US * (i + 0.5) / steps, 2, steps + 2 + i) for i in range(steps)]
    while left:
        best = None
        for link in free:
            ready = [
                (max(free[link], here[messages[i][2]]), -tail(i), i)
                for i in left
                if messages[i][0] == link and messages[i][2] in here
            ]
            if ready:
                first = min(ready)[0]
                pick = min((r for r in ready if r[0] <= first), key=lambda r: r[1:])
                if best is None or pick[0] < best[0]:
                    best = (pick[0], link, pick[2])
        begin, link, index = best
        left.remove(index)
        free[link] = begin + cost[index]
        key = messages[index][1]
        arrive = free[link] + HOP_US
        events.append((max(here[messages[index][2]] + 0.01, begin - 0.9 * UNIT_US), 1, index))
        events.append((arrive, 0, index))
        here[key] = max(here.get(key, 0.0), arrive)
    return messages, sorted(events)


def spread_kernel(
    gate_m, up_m, down_m, gate_g, up_g, down_g, gate_w, up_w, down_w, transform_in,
    gate_n, up_n, down_n, early, late, coefs,
    m0, m1, m2, g0, g1, g2, w0, w1, w2, transform, packed, rows, totals, lows, bands,
    peers, mine, loaded, stored, received, own, band_sent, band_received, sent, sent_c, side_sent, side_sent_c,
    side_received, side_received_c,
):
    loads = [
        pltpu.make_async_copy(a, b, loaded.at[i])
        for i, (a, b) in enumerate(
            zip(
                (gate_w, up_w, down_w, gate_m, up_m, down_m, gate_g, up_g, down_g, transform_in),
                (w0, w1, w2, m0, m1, m2, g0, g1, g2, transform),
            )
        )
    ]
    for load in loads:
        load.start()
    stores = [
        pltpu.make_async_copy(a, b, stored.at[i])
        for i, (a, b) in enumerate(((m0, gate_n), (m1, up_n), (m2, down_n)))
    ]
    replica, shard = lax.axis_index("replica"), lax.axis_index("fsdp")
    z, lo = lax.div(replica, 2), lax.rem(replica, 2)
    hi, y, core = lax.div(shard, 8), lax.rem(lax.div(shard, 2), 4), lax.rem(shard, 2)
    device = lambda z, lo, hi, y, core: (2 * z + lo, 8 * hi + 2 * y + core)
    turn = lambda at, by: lax.rem(at + by, 4)
    target = {
        "ym": device(z, lo, hi, turn(y, 1), core),
        "yp": device(z, lo, hi, turn(y, 3), core),
        "xc": device(z, 1 - lo, 1 - hi, y, core),
        "xi": device(z, 1 - lo, hi, y, core),
        "zm": device(turn(z, 1), lo, hi, y, core),
        "zp": device(turn(z, 3), lo, hi, y, core),
    }
    sibling = device(z, lo, hi, y, 1 - core)
    fellows = [
        device(turn(z, dz), lo if same else 1 - lo, hi, y, core)
        for dz in range(4)
        for same in (True, False)
        if not (dz == 0 and same)
    ]

    barrier = pltpu.get_barrier_semaphore()
    partners = [target["ym"], target["yp"], target["xc"], sibling] + fellows
    for partner in partners:
        pl.semaphore_signal(barrier, 1, device_id=partner, device_id_type=MESH)

    chunks = [pl.ds(at, STEP) for at in range(0, ENTRIES, STEP)]

    def lay(block, gate, up, down):
        @pl.when(core == 0)
        def _():
            block[0:108, :] = gate
            block[108:112, :] = down[16:20]
            block[112:220, :] = up
            block[220:224, :] = jnp.zeros_like(down[0:4])
            block[224:240, :] = down[0:16]

        @pl.when(core == 1)
        def _():
            block[0:4, :] = down[0:4]
            block[4:112, :] = gate
            block[112:116, :] = jnp.zeros_like(down[0:4])
            block[116:224, :] = up
            block[224:240, :] = down[4:20]

    for load in loads[:3]:
        load.wait()
    for chunk in chunks:
        lay(rows, *(w[:, chunk].astype(F32) for w in (w0, w1, w2)))
        packed[:, chunk] = rows[...].astype(BF16)
    pl.semaphore_wait(barrier, len(partners))

    groups = ENTRIES // 128
    windows = ((m0, g0, 0, 108), (m1, g1, 112, 108), (m2, g2, 224, 20))

    def accumulate(window, chunk):
        momentum, gradient, at, tiles = windows[window]
        if chunk == 0:
            loads[3 + window].wait()
            loads[6 + window].wait()
            if window == 0:
                loads[9].wait()
        pieces = []
        for group in range(chunk * STEP // 128, (chunk + 1) * STEP // 128):
            line = pl.ds(group, tiles, stride=groups)
            piece = 0.999 * momentum[line, :] + gradient[0, :, pl.ds(128 * group, 128)].astype(F32)
            momentum[line, :] = piece
            pieces.append(piece)
        total = None
        for part in head_tail(jnp.concatenate(pieces, axis=1)):
            product = lax.dot_general(
                part,
                transform[COEFS : 3 * COEFS, chunks[chunk]],
                (((1,), (1,)), ((), ())),
                preferred_element_type=F32,
            )
            total = product if total is None else total + product
        spot = pl.ds(at, tiles)
        totals[spot, :] = total if chunk == 0 else totals[spot, :] + total

    def finish_bands():
        both = []
        for _, _, at, tiles in windows:
            total = totals[pl.ds(at, tiles), :]
            both.append(jnp.concatenate(head_tail(total[:, :COEFS] + total[:, COEFS:]), axis=1).astype(F32))
            totals[pl.ds(at, tiles), :] = both[-1]
        lay(lows, *both)
        lows[ROWS:BAND_ROWS, :] = jnp.zeros((BAND_ROWS - ROWS, 2 * COEFS), F32)
        bands[...] = lows[...].astype(BF16)
        for fellow in fellows:
            remote(bands, peers.at[replica], band_sent, band_received, fellow).start()

    def remove(window, chunk):
        momentum, _, at, tiles = windows[window]
        both = totals[pl.ds(at, tiles), :].astype(BF16)
        twice = jnp.concatenate([both, both], axis=1)
        removed = jnp.dot(twice, transform[:, chunks[chunk]], preferred_element_type=F32)
        for part in range(STEP // 128):
            line = pl.ds(chunk * STEP // 128 + part, tiles, stride=groups)
            momentum[line, :] = momentum[line, :] - removed[:, 128 * part : 128 * (part + 1)]
        if chunk == len(chunks) - 1:
            stores[window].start()

    def remote(source, dest, send, receive, to):
        return pltpu.make_async_remote_copy(
            src_ref=source, dst_ref=dest, send_sem=send, recv_sem=receive, device_id=to, device_id_type=MESH
        )

    block_at = {
        (dx, dy): 8 * (hi if dx == 0 else 1 - hi) + 2 * turn(y, dy) + core for dx in range(2) for dy in range(4)
    }
    parity = (lo, 1 - lo)

    def place(array_rows, key, half):
        kind = key[0]
        columns = slice(None) if half is None else pl.ds(half * (ENTRIES // 2), ENTRIES // 2)
        if kind == "E":
            start = 32 * turn(z, key[1]) + 16 * parity[key[2]]
        elif kind == "D":
            start = EARLY + 48 * parity[key[1]] + 16 * key[2]
        elif kind == "H":
            start = 224
            columns = pl.ds(pl.multiple_of((ENTRIES // 2) * parity[key[1]], 128), ENTRIES // 2)
        else:
            return pl.ds(pl.multiple_of(128 * parity[key[1]], 16), 128), slice(None)
        return (pl.ds(start if isinstance(start, int) else pl.multiple_of(start, 16), 16), columns)

    part = lambda unit: early if unit[0] == "E" else late
    rows_in = lambda unit, rows: rows if unit[0] == "E" else pl.ds(rows.start - EARLY, rows.size)

    def refs(key, half):
        dx, dy, unit = key
        rows, columns = place(None, unit, half)
        block = block_at[(dx, dy)]
        if unit[0] == "C":
            here = coefs.at[block, rows, columns]
            return (mine.at[rows, columns] if (dx, dy) == (0, 0) else here), here
        if (dx, dy) == (0, 0):
            return packed.at[rows, columns], part(unit).at[block, rows_in(unit, rows), columns]
        here = part(unit).at[block, rows_in(unit, rows), columns]
        return here, here

    messages, events = plan()
    slices = [functools.partial(accumulate, w, c) for w in range(3) for c in range(len(chunks))]
    slices += [finish_bands, lambda: average()]
    slices += [functools.partial(remove, w, c) for w in range(3) for c in range(len(chunks))]
    me = block_at[(0, 0)]
    halves = ((packed.at[0:EARLY], early.at[me]), (packed.at[EARLY:ROWS], late.at[me]))
    own_copies = [pltpu.make_async_copy(a, b, own.at[i]) for i, (a, b) in enumerate(halves)]
    own_coefs = pltpu.make_async_copy(mine, coefs.at[me], own.at[2])

    def send(index):
        link, key, key_there, half = messages[index]
        source, dest = refs(key_there, half)
        is_coefs = key[2][0] == "C"
        which = sent_c if is_coefs else sent.at[int(key[2][0] != "E")]
        remote(source, dest, which, received.at[index], target[link]).start()

    def take(index):
        link, key, _, columns = messages[index]
        _, dest = refs(key, columns)
        is_coefs = key[2][0] == "C"
        remote(dest, dest, sent_c, received.at[index], target[link]).wait_recv()
        half = int(key[2][0] != "E")
        remote(
            dest,
            dest,
            side_sent_c if is_coefs else side_sent.at[half],
            side_received_c if is_coefs else side_received.at[half],
            sibling,
        ).start()

    def average():
        peers[replica] = bands[...]
        remote(peers.at[0:7], peers.at[0:7], band_sent, band_received, sibling).wait_recv()
        total = peers[0].astype(F32)
        for each in range(1, 8):
            total = total + peers[each].astype(F32)
        averaged = (total[:, :COEFS] + total[:, COEFS:]) / 8.0
        square = jnp.sum(averaged * averaged, axis=1, keepdims=True) / ENTRIES
        head, tail = head_tail(-0.5 * averaged / jnp.sqrt(square + 1e-06))
        mine[...] = jnp.concatenate([head, tail], axis=1)
        own_coefs.start()
        remote(mine, coefs.at[me], side_sent_c, side_received_c, sibling).start()

    first = True
    for when, kind, index in events:
        if kind == 1:
            send(index)
            continue
        if first:
            for copy in own_copies:
                copy.start()
            for i, (source, dest) in enumerate(halves):
                remote(source, dest, side_sent.at[i], side_received.at[i], sibling).start()
            first = False
        if kind == 2:
            slices[index]()
        else:
            take(index)

    for copy in own_copies:
        copy.wait()
    own_coefs.wait()
    for store in stores:
        store.wait()
    remote(peers.at[0:7], peers.at[0:7], band_sent, band_received, sibling).wait_send()
    for i, each in enumerate((early, late)):
        remote(each.at[0:7], each.at[0:7], sent.at[i], side_received.at[i], sibling).wait_send()
    remote(coefs.at[0:7], coefs.at[0:7], sent_c, side_received_c, sibling).wait_send()
    for i, each in enumerate((early, late)):
        remote(each.at[0:8], each.at[0:8], side_sent.at[i], side_received.at[i], sibling).wait()
    remote(coefs.at[0:8], coefs.at[0:8], side_sent_c, side_received_c, sibling).wait()


def spread(arrays, transform):
    dma = pltpu.SemaphoreType.DMA
    lines = [a.reshape(-1, 128) for a in arrays[:3]]
    here = lambda a: pltpu.VMEM(a.shape, a.dtype)
    band = pltpu.VMEM((BAND_ROWS, 2 * COEFS), BF16)
    return pl.pallas_call(
        spread_kernel,
        name="spread",
        out_shape=tuple(jax.ShapeDtypeStruct(a.shape, F32) for a in lines)
        + (
            jax.ShapeDtypeStruct((16, EARLY, ENTRIES), BF16),
            jax.ShapeDtypeStruct((16, ROWS - EARLY, ENTRIES), BF16),
            jax.ShapeDtypeStruct((16, BAND_ROWS, 2 * COEFS), BF16),
        ),
        in_specs=[ANY] * 10,
        out_specs=(ANY,) * 6,
        scratch_shapes=[here(a) for a in (*lines, *arrays[3:], transform)]
        + [
            pltpu.VMEM((ROWS, ENTRIES), BF16),
            pltpu.VMEM((ROWS, STEP), F32),
            pltpu.VMEM((BAND_ROWS, 2 * COEFS), F32),
            pltpu.VMEM((BAND_ROWS, 2 * COEFS), F32),
            band,
            pltpu.VMEM((8, BAND_ROWS, 2 * COEFS), BF16),
            band,
            dma((10,)),
            dma((3,)),
            dma((len(plan_messages()),)),
            dma((3,)),
        ]
        + [dma] * 2
        + [dma((2,)), dma, dma((2,)), dma, dma((2,)), dma],
        compiler_params=pltpu.CompilerParams(
            collective_id=0, has_side_effects=True, vmem_limit_bytes=16 * 2**20
        ),
    )(*in_hbm(*lines, *arrays[3:], transform))


QUAD = 4
WIDTH = 1024


def refresh_kernel(
    early, late, coefs, transform, gate_m, up_m, down_m, gate, up, down, gate_n, up_n, down_n
):
    gate_n[...] = gate_m[...]
    up_n[...] = up_m[...]
    down_n[...] = down_m[...]
    low_half = lax.broadcasted_iota(jnp.int32, (8, 256), 0) < 4
    for at in range(0, WIDTH, 256):
        chunk = pl.ds(at, 256)
        gates, ups, downs = [], [], []

        def renewed(each):
            both = coefs[each, 0:ROWS, :]
            twice = jnp.concatenate([both, both], axis=1)
            update = jnp.dot(twice, transform[:, chunk], preferred_element_type=F32)
            return (1.0 - 0.5 * 0.1) * jnp.concatenate(
                [early[each, :, chunk].astype(F32), late[each, :, chunk].astype(F32)], axis=0
            ) + update

        for pair in range(QUAD // 2):
            even, odd = renewed(2 * pair), renewed(2 * pair + 1)
            join = lambda a, b: jnp.where(low_half, a, b)
            gates += [even[0:104], join(even[104:112], odd[0:8]), odd[8:112]]
            ups += [even[112:216], join(even[216:224], odd[112:120]), odd[120:224]]
            downs += [
                even[224:240],
                join(pltpu.roll(even[104:112], 4, 0), pltpu.roll(odd[0:8], 4, 0)),
                odd[224:240],
            ]
        gate[:, chunk] = jnp.concatenate(gates, axis=0).astype(BF16)
        up[:, chunk] = jnp.concatenate(ups, axis=0).astype(BF16)
        down[:, chunk] = jnp.concatenate(downs, axis=0).astype(BF16)


def refresh(early, late, coefs, transform, moments):
    whole = lambda rows: jax.ShapeDtypeStruct((16 * rows, ENTRIES), BF16)
    out = lambda rows: pl.BlockSpec((QUAD * rows, WIDTH), lambda g, c: (g, c))
    steps = (16 // QUAD) * (ENTRIES // WIDTH)
    moment_specs = tuple(
        pl.BlockSpec((a.shape[0] // steps, 128), lambda g, c: (g * (ENTRIES // WIDTH) + c, 0)) for a in moments
    )
    return pl.pallas_call(
        refresh_kernel,
        name="refresh",
        grid=(16 // QUAD, ENTRIES // WIDTH),
        out_shape=(whole(108), whole(108), whole(20))
        + tuple(jax.ShapeDtypeStruct(a.shape, F32) for a in moments),
        in_specs=[
            pl.BlockSpec((QUAD, EARLY, WIDTH), lambda g, c: (g, 0, c)),
            pl.BlockSpec((QUAD, ROWS - EARLY, WIDTH), lambda g, c: (g, 0, c)),
            pl.BlockSpec((QUAD, BAND_ROWS, 2 * COEFS), lambda g, c: (g, 0, 0)),
            pl.BlockSpec((4 * COEFS, WIDTH), lambda g, c: (0, c)),
            *moment_specs,
        ],
        out_specs=(out(108), out(108), out(20)) + moment_specs,
        compiler_params=pltpu.CompilerParams(vmem_limit_bytes=14 * 2**20),
    )(early, late, coefs, transform, *moments)


def on_device(*arrays):
    transform = jnp.asarray(split_transform())
    *moments, early, late, coefs = spread(arrays, transform)
    *whole, gate_next, up_next, down_next = refresh(early, late, coefs, transform, moments)
    following = [a.reshape(b.shape) for a, b in zip((gate_next, up_next, down_next), arrays)]
    return (*following, *whole)


def solution(mesh):
    by_replica, by_shard = P("replica", "fsdp", None), P("fsdp", None)
    return jax.shard_map(
        on_device,
        mesh=mesh,
        in_specs=(by_replica,) * 6 + (by_shard,) * 3,
        out_specs=(by_replica,) * 3 + (P(),) * 3,
        check_vma=False,
    )
```

time: 135 us -> 94.1 us (0.70)
  local copies, waits for them, and re-layouts: 33.5 us -> 0.01 us
  Pallas kernels: 100 us -> 93.3 us
    unnamed x26 -> x2, local copies, waits for them, and re-layouts: 33.5 us -> 0.01 us
    pallas_call x2 -> x1, Pallas kernels: 83.4 us -> 75.7 us  [spread(): pl.pallas_call(spread_kernel, name='spread', out_shape=tuple((jax.ShapeDt...]
where the time goes in v2:
time: 94.1 us; the launch traced here: 94 us
  Pallas kernels  93.3 us (99%)
    pallas_call x1, Pallas kernels, spread(): pl.pallas_call(spread_kernel, name='spread', out_shape=tuple((jax.ShapeDt...  75.7 us
    pallas_call x1, Pallas kernels, refresh(): pl.pallas_call(refresh_kernel, name='refresh', grid=(16 // QUAD, ENTRIES...  17.6 us

profile of v2, /device:TPU:1, one launch (start us, length us, event | category | flops | bytes accessed | tf_op | source)
XLA Modules:
  0.0 94.0 jit_solution(7240957532067613866)
XLA Ops:
  0.6 0.0 copy-start
  0.6 75.7 %spread.1 = (f32[3456,128]{1,0:T(8,128)S(1)}, f32[3456,128]{1,0:T(8,128)S(1)}, f32[640,128]{1,0:T(8,128)S(1)}, bf16[16,128,4096]{2,1,0:T(8,128)(2,1)S(1)}, bf16[...) custom-call(f32[3456,128]{1,0:T(8,128)} %bitcast.6, f32[3456,128]{1,0:T(8,128)} %bitcast.7, ...), custom_call_target="tpu_custom_call" | custom-call | tf_op jit(solution)/shard_map/spread/pallas_call | solution.py:368
  76.4 0.0 copy-done
  76.4 17.6 %refresh.1 = (bf16[1728,4096]{1,0:T(8,128)(2,1)}, bf16[1728,4096]{1,0:T(8,128)(2,1)}, bf16[320,4096]{1,0:T(8,128)(2,1)}, f32[3456,128]{1,0:T(8,128)}, f32[3456,128]{1,0:T(8,128)}, /*index=5*/f32[640,128]{1,0:T(8,128)}) custom-call(bf16[16,128,4096]{2,1,0:T(8,128)(2,1)S(1)} %get-tuple-element.18.early, bf16[16,112,4096]{2,1,0:T(8,128)(2,1)S(1)} %get-tuple-element.19.late, ...), custom_call_target="tpu_custom_call" | custom-call | tf_op jit(solution)/shard_map/refresh/pallas_call | solution.py:446
Async XLA Ops:
  0.6 75.8 %copy-start = (bf16[256,4096]{1,0:T(8,128)(2,1)S(1)}, bf16[256,4096]{1,0:T(8,128)(2,1)}, u32[]{:S(2)}) copy-start(bf16[256,4096]{1,0:T(8,128)(2,1)} %constant.2.clone.transform_in.transform) | copy-start | bytes 6291460

commit v3 on v2

--- a/solution.py
+++ b/solution.py
@@ -45,33 +45,44 @@
     return head, (value - head.astype(F32)).astype(BF16)
 
 
-UNIT_US, HOP_US, BANDS_US = 2.85, 3.0, 22.0
-FOLD_US, REMOVE_US = 14.0, 24.0
-SIZE = {"E": 1.0, "D": 1.0, "H": 0.5, "C": 0.25}
+UNIT_US, HOP_US, BANDS_US = 2.85, 3.0, 30.0
+FOLD_US, REMOVE_US, REMOVE_FOR_US = 20.0, 24.0, 28.0
+AHEAD = 0.9
+SIZE = {"E": 1.0, "D": 1.0, "H": 0.5, "C": 0.25, "Q": 0.125}
+QUARTERED = (1, 3)
 
 
 def plan_messages():
     out = []
     band = lambda q: [("E", 0, q)] + [("D", q, k) for k in range(3)] + [("H", q), ("C", q)]
+    add = lambda link, key, there, half=None, after=None: out.append((link, key, there, half, after or (there,)))
     for link, near in (("ym", 3), ("yp", 1)):
         for unit in band(0) + band(1) + [("E", dz, 1) for dz in (1, 2, 3)]:
-            out.append((link, (0, near, unit), (0, 0, unit), None))
+            add(link, (0, near, unit), (0, 0, unit))
     for link, near, q, dz, half in (("ym", 3, 0, 1, 0), ("yp", 1, 1, 3, 1)):
         for unit in band(q) + [("E", dz, 1)]:
-            out.append((link, (0, 2, unit), (0, near, unit), None))
-        out.append((link, (0, 2, ("E", 2, 1)), (0, near, ("E", 2, 1)), half))
+            add(link, (0, 2, unit), (0, near, unit))
+        add(link, (0, 2, ("E", 2, 1)), (0, near, ("E", 2, 1)), half)
     for dy in range(4):
         for own, other in zip(band(0), band(1)):
-            out.append(("xc", (1, dy, own), (0, dy, other), None))
-            out.append(("xi", (1, dy, other), (1, dy, own), None))
+            if own[0] == "C":
+                add("xc", (1, dy, own), (0, dy, other))
+                add("xc", (1, dy, other), (0, dy, own))
+            elif own[0] == "H" and dy in QUARTERED:
+                add("xc", (1, dy, ("Q", 0, 0)), (0, dy, ("Q", 0, 1)), None, ((0, dy, own), (0, dy, other)))
+                add("xi", (1, dy, ("Q", 0, 1)), (1, dy, ("Q", 0, 0)))
+            else:
+                add("xc", (1, dy, own), (0, dy, other))
+                add("xi", (1, dy, other), (1, dy, own))
     for link, dz, q, half in (("zm", 3, 0, 0), ("zp", 1, 1, 1)):
         for dy in (1, 2, 3):
-            out.append((link, (0, dy, ("E", dz, 0)), (0, dy, ("E", 0, 0)), None))
-            out.append((link, (0, dy, ("E", 2, 0)), (0, dy, ("E", dz, 0)), half))
+            add(link, (0, dy, ("E", dz, 0)), (0, dy, ("E", 0, 0)))
+            add(link, (0, dy, ("E", 2, 0)), (0, dy, ("E", dz, 0)), half)
         for dy in range(4):
-            for each in (0, 1):
-                out.append((link, (1, dy, ("E", dz, each)), (1, dy, ("E", 0, each)), None))
-            out.append((link, (1, dy, ("E", 2, q)), (1, dy, ("E", dz, q)), None))
+            for kind in ("E", "Q") if dy in QUARTERED else ("E",):
+                for each in (0, 1):
+                    add(link, (1, dy, (kind, dz, each)), (1, dy, (kind, 0, each)))
+                add(link, (1, dy, (kind, 2, q)), (1, dy, (kind, dz, q)))
     return out
 
 
@@ -79,7 +90,8 @@
     messages = plan_messages()
     users = {}
     for index, message in enumerate(messages):
-        users.setdefault(message[2], []).append(index)
+        for source in message[4]:
+            users.setdefault(source, []).append(index)
     cost = [SIZE[m[1][2][0]] * (0.5 if m[3] is not None else 1.0) * UNIT_US for m in messages]
     known = {}
 
@@ -91,33 +103,34 @@
 
     here = {}
     for message in messages:
-        if message[2][:2] == (0, 0):
-            here[message[2]] = BANDS_US if message[2][2][0] == "C" else 0.0
+        for source in message[4]:
+            if source[:2] == (0, 0):
+                here[source] = BANDS_US if source[2][0] == "C" else 0.0
     free = dict.fromkeys(("ym", "yp", "xc", "xi", "zm", "zp"), 0.0)
     left = list(range(len(messages)))
     steps = 3 * (ENTRIES // STEP)
     events = [(FOLD_US * (i + 0.5) / steps, 2, i) for i in range(steps)]
     events += [(FOLD_US + 0.1, 2, steps), (BANDS_US - 0.5, 2, steps + 1)]
-    events += [(REMOVE_US + FOLD_US * (i + 0.5) / steps, 2, steps + 2 + i) for i in range(steps)]
+    events += [(REMOVE_US + REMOVE_FOR_US * (i + 0.5) / steps, 2, steps + 2 + i) for i in range(steps)]
     while left:
         best = None
         for link in free:
-            ready = [
-                (max(free[link], here[messages[i][2]]), -tail(i), i)
-                for i in left
-                if messages[i][0] == link and messages[i][2] in here
-            ]
+            ready = []
+            for i in left:
+                if messages[i][0] == link and all(source in here for source in messages[i][4]):
+                    at = max(here[source] for source in messages[i][4])
+                    ready.append((max(free[link], at), -tail(i), i, at))
             if ready:
                 first = min(ready)[0]
                 pick = min((r for r in ready if r[0] <= first), key=lambda r: r[1:])
                 if best is None or pick[0] < best[0]:
-                    best = (pick[0], link, pick[2])
-        begin, link, index = best
+                    best = (pick[0], link, pick[2], pick[3])
+        begin, link, index, at = best
         left.remove(index)
         free[link] = begin + cost[index]
         key = messages[index][1]
         arrive = free[link] + HOP_US
-        events.append((max(here[messages[index][2]] + 0.01, begin - 0.9 * UNIT_US), 1, index))
+        events.append((max(at + 0.01, begin - AHEAD * UNIT_US), 1, index))
         events.append((arrive, 0, index))
         here[key] = max(here.get(key, 0.0), arrive)
     return messages, sorted(events)
@@ -268,6 +281,9 @@
         elif kind == "H":
             start = 224
             columns = pl.ds(pl.multiple_of((ENTRIES // 2) * parity[key[1]], 128), ENTRIES // 2)
+        elif kind == "Q":
+            start = 224
+            columns = pl.ds(pl.multiple_of(1024 * turn(z, key[1]) + 512 * parity[key[2]], 128), 512)
         else:
             return pl.ds(pl.multiple_of(128 * parity[key[1]], 16), 128), slice(None)
         return (pl.ds(start if isinstance(start, int) else pl.multiple_of(start, 16), 16), columns)
@@ -297,14 +313,14 @@
     own_coefs = pltpu.make_async_copy(mine, coefs.at[me], own.at[2])
 
     def send(index):
-        link, key, key_there, half = messages[index]
+        link, key, key_there, half, _ = messages[index]
         source, dest = refs(key_there, half)
         is_coefs = key[2][0] == "C"
         which = sent_c if is_coefs else sent.at[int(key[2][0] != "E")]
         remote(source, dest, which, received.at[index], target[link]).start()
 
     def take(index):
-        link, key, _, columns = messages[index]
+        link, key, _, columns, _ = messages[index]
         _, dest = refs(key, columns)
         is_coefs = key[2][0] == "C"
         remote(dest, dest, sent_c, received.at[index], target[link]).wait_recv()
@@ -399,7 +415,7 @@
 
 
 QUAD = 4
-WIDTH = 1024
+WIDTH = 2048
 
 
 def refresh_kernel(
@@ -409,16 +425,18 @@
     up_n[...] = up_m[...]
     down_n[...] = down_m[...]
     low_half = lax.broadcasted_iota(jnp.int32, (8, 256), 0) < 4
+    first, left = QUAD * pl.program_id(0), WIDTH * pl.program_id(1)
     for at in range(0, WIDTH, 256):
         chunk = pl.ds(at, 256)
+        column = pl.ds(pl.multiple_of(left + at, 256), 256)
         gates, ups, downs = [], [], []
 
         def renewed(each):
-            both = coefs[each, 0:ROWS, :]
+            both = coefs[first + each, 0:ROWS, :]
             twice = jnp.concatenate([both, both], axis=1)
             update = jnp.dot(twice, transform[:, chunk], preferred_element_type=F32)
             return (1.0 - 0.5 * 0.1) * jnp.concatenate(
-                [early[each, :, chunk].astype(F32), late[each, :, chunk].astype(F32)], axis=0
+                [early[first + each, :, column].astype(F32), late[first + each, :, column].astype(F32)], axis=0
             ) + update
 
         for pair in range(QUAD // 2):
@@ -450,9 +468,9 @@
         out_shape=(whole(108), whole(108), whole(20))
         + tuple(jax.ShapeDtypeStruct(a.shape, F32) for a in moments),
         in_specs=[
-            pl.BlockSpec((QUAD, EARLY, WIDTH), lambda g, c: (g, 0, c)),
-            pl.BlockSpec((QUAD, ROWS - EARLY, WIDTH), lambda g, c: (g, 0, c)),
-            pl.BlockSpec((QUAD, BAND_ROWS, 2 * COEFS), lambda g, c: (g, 0, 0)),
+            VMEM,
+            VMEM,
+            VMEM,
             pl.BlockSpec((4 * COEFS, WIDTH), lambda g, c: (0, c)),
             *moment_specs,
         ],

time: 94.1 us -> 87.4 us (0.929)
  Pallas kernels: 93.3 us -> 86.6 us
    pallas_call x1, Pallas kernels: 75.7 us -> 72.2 us  [spread(): pl.pallas_call(spread_kernel, name='spread', out_shape=tuple((jax.ShapeDt...]
    pallas_call x1, Pallas kernels: 17.6 us -> 14.4 us  [refresh(): pl.pallas_call(refresh_kernel, name='refresh', grid=(16 // QUAD, ENTRIES...]
where the time goes in v3:
time: 87.4 us; the launch traced here: 87.3 us
  Pallas kernels  86.6 us (99%)
    pallas_call x1, Pallas kernels, spread(): pl.pallas_call(spread_kernel, name='spread', out_shape=tuple((jax.ShapeDt...  72.2 us
    pallas_call x1, Pallas kernels, refresh(): pl.pallas_call(refresh_kernel, name='refresh', grid=(16 // QUAD, ENTRIES...  14.4 us

profile of v3, /device:TPU:1, one launch (start us, length us, event | category | flops | bytes accessed | tf_op | source)
XLA Modules:
  0.0 87.3 jit_solution(3276730774029710413)
XLA Ops:
  0.6 0.0 copy-start
  0.6 72.2 %spread.1 = (f32[3456,128]{1,0:T(8,128)S(1)}, f32[3456,128]{1,0:T(8,128)S(1)}, f32[640,128]{1,0:T(8,128)S(1)}, bf16[16,128,4096]{2,1,0:T(8,128)(2,1)S(1)}, bf16[...) custom-call(f32[3456,128]{1,0:T(8,128)} %bitcast.6, f32[3456,128]{1,0:T(8,128)} %bitcast.7, ...), custom_call_target="tpu_custom_call" | custom-call | tf_op jit(solution)/shard_map/spread/pallas_call | solution.py:384
  72.9 0.0 copy-done
  72.9 14.4 %refresh.1 = (bf16[1728,4096]{1,0:T(8,128)(2,1)}, bf16[1728,4096]{1,0:T(8,128)(2,1)}, bf16[320,4096]{1,0:T(8,128)(2,1)}, f32[3456,128]{1,0:T(8,128)}, f32[3456,128]{1,0:T(8,128)}, /*index=5*/f32[640,128]{1,0:T(8,128)}) custom-call(bf16[16,128,4096]{2,1,0:T(8,128)(2,1)S(1)} %get-tuple-element.18.early, bf16[16,112,4096]{2,1,0:T(8,128)(2,1)S(1)} %get-tuple-element.19.late, ...), custom_call_target="tpu_custom_call" | custom-call | tf_op jit(solution)/shard_map/refresh/pallas_call | solution.py:464
Async XLA Ops:
  0.6 72.2 %copy-start = (bf16[256,4096]{1,0:T(8,128)(2,1)S(1)}, bf16[256,4096]{1,0:T(8,128)(2,1)}, u32[]{:S(2)}) copy-start(bf16[256,4096]{1,0:T(8,128)(2,1)} %constant.2.clone.transform_in.transform) | copy-start | bytes 6291460

commit v4 on v3

--- a/solution.py
+++ b/solution.py
@@ -421,9 +421,10 @@
 def refresh_kernel(
     early, late, coefs, transform, gate_m, up_m, down_m, gate, up, down, gate_n, up_n, down_n
 ):
-    gate_n[...] = gate_m[...]
-    up_n[...] = up_m[...]
-    down_n[...] = down_m[...]
+    step = pl.program_id(0) * pl.num_programs(1) + pl.program_id(1)
+    for source, dest in ((gate_m, gate_n), (up_m, up_n), (down_m, down_n)):
+        lines = dest.shape[0]
+        dest[...] = source[pl.ds(pl.multiple_of(step * lines, 8), lines), :]
     low_half = lax.broadcasted_iota(jnp.int32, (8, 256), 0) < 4
     first, left = QUAD * pl.program_id(0), WIDTH * pl.program_id(1)
     for at in range(0, WIDTH, 256):
@@ -434,7 +435,7 @@
         def renewed(each):
             both = coefs[first + each, 0:ROWS, :]
             twice = jnp.concatenate([both, both], axis=1)
-            update = jnp.dot(twice, transform[:, chunk], preferred_element_type=F32)
+            update = jnp.dot(twice, transform[:, column], preferred_element_type=F32)
             return (1.0 - 0.5 * 0.1) * jnp.concatenate(
                 [early[first + each, :, column].astype(F32), late[first + each, :, column].astype(F32)], axis=0
             ) + update
@@ -471,8 +472,8 @@
             VMEM,
             VMEM,
             VMEM,
-            pl.BlockSpec((4 * COEFS, WIDTH), lambda g, c: (0, c)),
-            *moment_specs,
+            VMEM,
+            *[VMEM] * len(moments),
         ],
         out_specs=(out(108), out(108), out(20)) + moment_specs,
         compiler_params=pltpu.CompilerParams(vmem_limit_bytes=14 * 2**20),

time: 87.4 us -> 87.1 us (level)
  no operation moved by 1% of the time
where the time goes in v4:
time: 87.1 us; the launch traced here: 87 us
  Pallas kernels  86.3 us (99%)
    pallas_call x1, Pallas kernels, spread(): pl.pallas_call(spread_kernel, name='spread', out_shape=tuple((jax.ShapeDt...  72.2 us
    pallas_call x1, Pallas kernels, refresh(): pl.pallas_call(refresh_kernel, name='refresh', grid=(16 // QUAD, ENTRIES...  14.1 us

profile of v4, /device:TPU:1, one launch (start us, length us, event | category | flops | bytes accessed | tf_op | source)
XLA Modules:
  0.0 87.0 jit_solution(3364965734095117524)
XLA Ops:
  0.6 0.0 copy-start
  0.6 72.2 %spread.1 = (f32[3456,128]{1,0:T(8,128)S(1)}, f32[3456,128]{1,0:T(8,128)S(1)}, f32[640,128]{1,0:T(8,128)S(1)}, bf16[16,128,4096]{2,1,0:T(8,128)(2,1)S(1)}, bf16[...) custom-call(f32[3456,128]{1,0:T(8,128)} %bitcast.6, f32[3456,128]{1,0:T(8,128)} %bitcast.7, ...), custom_call_target="tpu_custom_call" | custom-call | tf_op jit(solution)/shard_map/spread/pallas_call | solution.py:384
  72.9 0.0 copy-done
  72.9 14.1 %refresh.1 = (bf16[1728,4096]{1,0:T(8,128)(2,1)}, bf16[1728,4096]{1,0:T(8,128)(2,1)}, bf16[320,4096]{1,0:T(8,128)(2,1)}, f32[3456,128]{1,0:T(8,128)}, f32[3456,128]{1,0:T(8,128)}, /*index=5*/f32[640,128]{1,0:T(8,128)}) custom-call(bf16[16,128,4096]{2,1,0:T(8,128)(2,1)S(1)} %get-tuple-element.18.early, bf16[16,112,4096]{2,1,0:T(8,128)(2,1)S(1)} %get-tuple-element.19.late, ...), custom_call_target="tpu_custom_call" | custom-call | tf_op jit(solution)/shard_map/refresh/pallas_call | solution.py:465
Async XLA Ops:
  0.6 72.2 %copy-start = (bf16[256,4096]{1,0:T(8,128)(2,1)S(1)}, bf16[256,4096]{1,0:T(8,128)(2,1)}, u32[]{:S(2)}) copy-start(bf16[256,4096]{1,0:T(8,128)(2,1)} %constant.2.clone.transform_in.transform) | copy-start | bytes 6291460
